TPU v7x, 32 devices: a whole 2x2x4 slice. The times are simulated.
32 devices in a mesh: grp: 2 (over y), row: 4 (over z), ch: 2 (over x), sub: 2 (over core).
Axes of the slice: x: 2, y: 2, z: 4, core: 2. Of those that a mesh axis runs over, the one named last changes fastest.
Arguments:
- pair_act: bfloat16 [128, 256, 128], P('ch', ('grp', 'row'), 'sub'), parts along dimension 1, may hold values from -6 to 6
- token_mask: int32 [256], P('grp'), parts along dimension 0, may hold values 0 or 1
- norm_gain: float32 [128], replicated, may hold values from 0.1 to 1.9
- norm_shift: float32 [128], replicated, may hold values from -2.5 to 2.5
- proj_weight: bfloat16 [128, 256], replicated, may hold values from -0.5 to 0.5
- gate_weight: bfloat16 [128, 256], replicated, may hold values from -0.5 to 0.5
- outgate_weight: bfloat16 [128, 128], replicated, may hold values from -0.5 to 0.5
- post_gain: float32 [128], replicated, may hold values from 0.1 to 1.9
- post_shift: float32 [128], replicated, may hold values from -2.5 to 2.5
- out_weight: bfloat16 [128, 128], replicated, may hold values from -0.5 to 0.5
Outputs:
- update: bfloat16 [128, 256, 128], P('ch', ('grp', 'row'), 'sub'), parts along dimension 1
There are 2 independent parts, one for each index of `grp`. A program takes and returns all parts, laid end to end along the dimension named above; an argument that names none is the same for every part. Nothing has to cross between parts.
All inputs are finite; a program needn't handle non-finite values.
Results may differ from a plain program's by a relative error of at most 0.0062.
Values may be sent and summed in bfloat16 or wider, within the bound.
A program may use at most 64 MiB of HBM per device.

v0:
```python
import jax
import jax.numpy as jnp
from jax import lax
from jax.sharding import PartitionSpec as P


def layer_norm(values, gain, shift):
    widened = values.astype(jnp.float32)
    average = jnp.mean(widened, axis=0, keepdims=True)
    centered = widened - average
    variance = jnp.mean(centered * centered, axis=0, keepdims=True)
    scaled = centered * lax.rsqrt(variance + 1e-05)
    spread = (gain.shape[0],) + (1,) * (values.ndim - 1)
    return (scaled * gain.reshape(spread) + shift.reshape(spread)).astype(jnp.bfloat16)


def gated_inputs(normed, weights, pair_mask, hidden):
    projected = jnp.einsum("ce,c...->e...", weights, normed, preferred_element_type=jnp.float32)
    left_panel = (
        projected[:hidden] * jax.nn.sigmoid(projected[2 * hidden : 3 * hidden]) * pair_mask
    ).astype(jnp.bfloat16)
    right_panel = (
        projected[hidden : 2 * hidden]
        * jax.nn.sigmoid(projected[3 * hidden : 4 * hidden])
        * pair_mask
    ).astype(jnp.bfloat16)
    outgate = jax.nn.sigmoid(projected[4 * hidden :])
    return (left_panel, right_panel, outgate)


def contract(left_panel, right_panel):
    partial_sums = jnp.einsum(
        "hik,hjk->hij",
        left_panel,
        lax.all_gather(right_panel, "row", axis=1, tiled=True),
        preferred_element_type=jnp.float32,
    )
    return lax.psum_scatter(partial_sums, "sub", scatter_dimension=2, tiled=True).astype(
        jnp.bfloat16
    )


def body(
    pair_act,
    token_mask,
    norm_gain,
    norm_shift,
    proj_weight,
    gate_weight,
    outgate_weight,
    post_gain,
    post_shift,
    out_weight,
):
    slab_rows = pair_act.shape[1]
    slab_cols = pair_act.shape[2]
    hidden = out_weight.shape[0]
    channels = out_weight.shape[1]
    chan_count = lax.axis_size("ch")
    chan_index = lax.axis_index("ch")
    masked = token_mask.astype(jnp.float32)
    row_mask = lax.dynamic_slice_in_dim(masked, lax.axis_index("row") * slab_rows, slab_rows, 0)
    col_start = lax.axis_index("sub") * slab_cols
    gathered = lax.all_gather(pair_act, "ch", axis=0, tiled=True)
    normed = layer_norm(gathered, norm_gain, norm_shift)
    col_mask = lax.dynamic_slice_in_dim(masked, col_start, slab_cols, 0)
    pair_mask = row_mask[:, None] * col_mask[None, :]
    hid_part = hidden // chan_count
    out_part = channels // chan_count
    hid_start = chan_index * hid_part
    out_start = chan_index * out_part
    weights = jnp.concatenate(
        [
            lax.dynamic_slice_in_dim(proj_weight, hid_start, hid_part, 1),
            lax.dynamic_slice_in_dim(proj_weight, hidden + hid_start, hid_part, 1),
            lax.dynamic_slice_in_dim(gate_weight, hid_start, hid_part, 1),
            lax.dynamic_slice_in_dim(gate_weight, hidden + hid_start, hid_part, 1),
            lax.dynamic_slice_in_dim(outgate_weight, out_start, out_part, 1),
        ],
        axis=1,
    )
    left_panel, right_panel, outgate = gated_inputs(normed, weights, pair_mask, hid_part)
    triangle = contract(left_panel, right_panel)
    all_hidden = lax.all_gather(triangle, "ch", axis=0, tiled=True)
    post = layer_norm(all_hidden, post_gain, post_shift)
    out_slice = lax.dynamic_slice_in_dim(out_weight, out_start, out_part, 1)
    projected_out = jnp.einsum("hc,hij->cij", out_slice, post, preferred_element_type=jnp.float32)
    return (projected_out * outgate).astype(jnp.bfloat16)


def solution(mesh):
    placed = (P("ch", ("grp", "row"), "sub"), P("grp"), P(), P(), P(), P(), P(), P(), P(), P())
    return jax.shard_map(
        body, mesh=mesh, in_specs=placed, out_specs=P("ch", ("grp", "row"), "sub"), check_vma=False
    )
```

profile of v0, /device:TPU:0, one launch (start us, length us, event | category | flops | bytes accessed | tf_op | source)
XLA Modules:
  0.0 136.5 jit_solution(8530916873722835195)
XLA Ops:
  6.5 0.7 convert_element_type.29
  7.2 0.1 dynamic_slice.31
  7.3 0.1 dynamic_slice.30
  7.4 0.8 constant_dynamic-slice_fusion
  8.2 0.1 copy.44
  8.3 0.9 constant_dynamic-slice_fusion.1
  9.2 0.1 copy.43
  9.3 0.1 copy.42
  9.4 0.1 copy.40
  9.5 0.1 copy.41
  9.7 15.8 %all_gather.9 = bf16[128,32,64]{2,1,0:T(8,128)(2,1)S(1)} all-gather(bf16[64,32,64]{2,1,0:T(8,128)(2,1)} %param.10), channel_id=1, replica_groups=mesh['grp'=2,'row'=4,'ch'=2,'sub'=2] {'ch'}, dimensions={0}, use_global_device_ids=true | all-gather | bytes 786432 | tf_op jit(solution)/shard_map/all_gather | solution.py:64
  25.4 0.3 convert_reduce_fusion.1
  25.7 0.4 fusion.8
  26.1 0.4 fusion.11
  26.6 1.9 %copy.29 = bf16[128,32,64]{0,2,1:T(8,128)(2,1)} copy(bf16[128,32,64]{2,1,0:T(8,128)(2,1)S(1)} %fusion.11) | data formatting | bytes 1048576 | tf_op jit(solution)/shard_map/convert_element_type | solution.py:14
  28.6 1.6 %fusion.34 = f32[320,2048]{0,1:S(1)} fusion(bf16[128,320]{0,1:T(8,128)(2,1)S(1)} %constant_dynamic-update-slice_fusion, bf16[128,2048]{0,1:T(8,128)(2,1)} %bitcast.15), kind=kOutput, calls=%fused_computation.57 | convolution fusion | flops 167772160 | bytes 3227648
  30.2 1.9 %fusion.30 = (bf16[64,32,64]{0,2,1:T(8,128)(2,1)}, bf16[64,32,64]{0,2,1:T(8,128)(2,1)}) fusion(f32[320,32,64]{0,2,1:T(8,128)S(1)} %bitcast.11, f32[32,64]{1,0:T(8,128)S(1)} %broadcast_multiply_fusion), kind=kLoop, calls=%fused_computation.38 | loop fusion | flops 1572864 | bytes 2629632 | tf_op jit(solution)/shard_map/convert_element_type | solution.py:26
  32.0 2.1 %copy.30 = bf16[64,32,64]{2,0,1:T(8,128)(2,1)} copy(bf16[64,32,64]{0,2,1:T(8,128)(2,1)} %get-tuple-element.5) | data formatting | bytes 524288 | tf_op jit(solution)/shard_map/convert_element_type | solution.py:26
  34.2 2.5 %copy.31 = bf16[64,32,64]{2,1,0:T(8,128)(2,1)} copy(bf16[64,32,64]{0,2,1:T(8,128)(2,1)} %get-tuple-element.6) | data formatting | bytes 524288 | tf_op jit(solution)/shard_map/convert_element_type | solution.py:21
  36.7 45.0 %all-gather.2.cloned.1.call-done = bf16[64,128,64]{2,0,1:T(8,128)(2,1)} async-done(((bf16[64,32,64]{2,0,1:T(8,128)(2,1)}), bf16[64,128,64]{2,0,1:T(8,128)(2,1)}) %all-gather.2.cloned.1.call-update) | async-done | bytes 1048592 | tf_op jit(solution)/shard_map/all_gather | solution.py:35
  81.7 4.6 %fusion.12 = f32[64,32,128]{2,1,0:T(8,128)} fusion(bf16[64,32,64]{2,1,0:T(8,128)(2,1)} %copy.31, bf16[64,128,64]{2,0,1:T(8,128)(2,1)} %all-gather.2.cloned.1.call-done), kind=kOutput, calls=%fused_computation.16 | convolution fusion | flops 33554432 | bytes 2359296 | tf_op jit(solution)/shard_map/hik,hjk->hij/dot_general | solution.py:32
  86.3 5.4 %copy.37 = f32[64,32,128]{1,0,2:T(8,128)} copy(f32[64,32,128]{2,1,0:T(8,128)} %fusion.12) | data formatting | bytes 2097152
  91.6 4.4 %reshape.62 = f32[128,2048]{1,0:T(8,128)} reshape(f32[128,64,32]{2,1,0:T(8,128)} %bitcast.13) | data formatting | bytes 2097152
  96.1 7.4 %reduce-scatter.4.cloned.1.call-done = f32[64,2048]{1,0:T(8,128)} async-done(((f32[128,2048]{1,0:T(8,128)}), f32[64,2048]{1,0:T(8,128)}) %reduce-scatter.4.cloned.1.call-update) | async-done | bytes 524304
  103.5 2.7 %reshape.63 = bf16[64,64,32]{2,1,0:T(8,128)(2,1)} reshape(f32[64,2048]{1,0:T(8,128)} %reduce-scatter.4.cloned.1.call-done) | data formatting | bytes 786432
  106.2 3.0 %copy.38 = bf16[64,32,64]{2,1,0:T(8,128)(2,1)} copy(bf16[64,32,64]{1,0,2:T(8,128)(2,1)} %bitcast.14) | data formatting | bytes 524288
  109.3 15.3 %all_gather.11 = bf16[128,32,64]{2,1,0:T(8,128)(2,1)S(1)} all-gather(bf16[64,32,64]{2,1,0:T(8,128)(2,1)} %copy.38), channel_id=1, replica_groups=mesh['grp'=2,'row'=4,'ch'=2,'sub'=2] {'ch'}, dimensions={0}, use_global_device_ids=true | all-gather | bytes 786432 | tf_op jit(solution)/shard_map/all_gather | solution.py:84
  124.6 0.3 convert_reduce_fusion
  124.9 0.4 fusion.4
  125.3 0.4 fusion.7
  125.7 1.4 %fusion.14 = bf16[64,32,64]{0,2,1:T(8,128)(2,1)} fusion(f32[320,32,64]{0,2,1:T(8,128)S(1)} %bitcast.12, bf16[128,32,64]{2,1,0:T(8,128)(2,1)S(1)} %fusion.7, bf16[128,128]{1,0:T(8,128)(2,1)S(1)} %copy-done, s32[]{:T(128)S(6)} %select_n.18), kind=kOutput, calls=%fused_computation.19 | convolution fusion | flops 34209792 | bytes 1343492 | tf_op jit(solution)/shard_map/hc,hij->cij/dot_general | solution.py:87
  127.1 2.5 %copy.35 = bf16[64,32,64]{2,1,0:T(8,128)(2,1)} copy(bf16[64,32,64]{0,2,1:T(8,128)(2,1)} %fusion.14) | data formatting | bytes 524288 | tf_op jit(solution)/shard_map/convert_element_type | solution.py:88
  (24 shorter events, 0.2 us)
Async XLA Ops:
  6.5 119.2 %copy-start = (bf16[128,128]{1,0:T(8,128)(2,1)S(1)}, bf16[128,128]{1,0:T(8,128)(2,1)}, u32[]{:S(2)}) copy-start(bf16[128,128]{1,0:T(8,128)(2,1)} %param.19) | copy-start | bytes 98308
  6.5 75.1 %all-gather.2.cloned.1.call-start = ((), (), s32[]{:S(2)}) async-start(), calls=%async_computation.1 | async-start | bytes 2621440 | tf_op jit(solution)/shard_map/all_gather | solution.py:35
  8.3 17.8 %copy-start.1 = (f32[128]{0:T(128)S(1)}, f32[128]{0:T(128)}, u32[]{:S(2)}) copy-start(f32[128]{0:T(128)} %param.13) | copy-start | bytes 1540
  8.3 17.8 %copy-start.2 = (f32[128]{0:T(128)S(1)}, f32[128]{0:T(128)}, u32[]{:S(2)}) copy-start(f32[128]{0:T(128)} %param.12) | copy-start | bytes 1540
  34.1 69.4 %reduce-scatter.4.cloned.1.call-start = ((), (), s32[]{:S(2)}) async-start(), calls=%async_computation.2 | async-start | bytes 1572864
  109.2 16.0 %copy-start.3 = (f32[128]{0:T(128)S(1)}, f32[128]{0:T(128)}, u32[]{:S(2)}) copy-start(f32[128]{0:T(128)} %param.18) | copy-start | bytes 1540
  109.3 16.0 %copy-start.4 = (f32[128]{0:T(128)S(1)}, f32[128]{0:T(128)}, u32[]{:S(2)}) copy-start(f32[128]{0:T(128)} %param.17) | copy-start | bytes 1540
Sparse Core Ops, SparseCore 0:
  34.2 47.3 all-gather.1
  96.2 7.2 reduce-scatter.3
where the time goes:
time: 137 us
  waiting for transfers between devices  52.4 us (38%)
  blocking collectives  31.1 us (23%)
  local copies, waits for them, and re-layouts  27 us (20%)
  between operations  13.6 us (10%)
  matrix products  7.58 us (6%)
  other arithmetic  4.8 us (4%)
    all_gather x1, waiting for transfers between devices, contract(): lax.all_gather(right_panel, 'row', axis=1, tiled=True)  45 us
    unnamed x23, local copies, waits for them, and re-layouts  16.1 us
    all_gather x1, blocking collectives, body(): gathered = lax.all_gather(pair_act, 'ch', axis=0, tiled=True)  15.8 us
    all_gather x1, blocking collectives, body(): all_hidden = lax.all_gather(triangle, 'ch', axis=0, tiled=True)  15.3 us
    unnamed x3, waiting for transfers between devices  7.43 us
    dot_general x1, matrix products, contract(): jnp.einsum('hik,hjk->hij', left_panel, lax.all_gather(right_panel, 'row',...  4.58 us
  transfers between devices with their start and end apart: 2, of which 2 were waited for; matrix products, arithmetic and copies ran while one was open for 2% of the time, Pallas kernels for 0%

commit v1 on v0

--- a/solution.py
+++ b/solution.py
@@ -1,6 +1,10 @@
+import functools
+
 import jax
 import jax.numpy as jnp
 from jax import lax
+from jax.experimental import pallas as pl
+from jax.experimental.pallas import tpu as pltpu
 from jax.sharding import PartitionSpec as P
 
 
@@ -88,8 +92,319 @@
     return (projected_out * outgate).astype(jnp.bfloat16)
 
 
+MESH = pl.DeviceIdType.MESH
+LANES = 128
+HALF = 64
+CHUNKS = 4
+
+
+def column(row):
+    return jnp.transpose(jnp.broadcast_to(row.astype(jnp.float32), (LANES, LANES)))
+
+
+def spread_gain(panel, lanes):
+    return jnp.concatenate([panel] * (lanes // LANES), axis=1)
+
+
+def swish_gate(values):
+    return 0.5 * jnp.tanh(0.5 * values) + 0.5
+
+
+def normalise(values, gain, shift):
+    average = jnp.mean(values, axis=0, keepdims=True)
+    centered = values - average
+    variance = jnp.mean(centered * centered, axis=0, keepdims=True)
+    scaled = centered * lax.rsqrt(variance + 1e-05)
+    return (scaled * gain + shift).astype(jnp.bfloat16)
+
+
+def fused_kernel(
+    rows,
+    x_ref,
+    mask_ref,
+    norm_gain,
+    norm_shift,
+    proj_ref,
+    gate_ref,
+    outgate_ref,
+    post_gain,
+    post_shift,
+    out_weight,
+    o_ref,
+    x_all,
+    weights,
+    turned,
+    columns,
+    gate_keep,
+    send_buf,
+    recv_buf,
+    wide,
+    panels,
+    tri_wide,
+    tri_send,
+    tri_all,
+    local_sem,
+    x_send,
+    x_recv,
+    a_send,
+    a_recv,
+    t_send,
+    t_recv,
+    f_send,
+    f_recv,
+):
+    row = lax.axis_index("row")
+    ch = lax.axis_index("ch")
+    sub = lax.axis_index("sub")
+    dests = 2 * rows
+    me = row * 2 + sub
+    other_ch = 1 - ch
+    tiles = x_ref.shape[1] // LANES
+    per = tiles // CHUNKS
+    width = per * LANES
+
+    def peer(offset):
+        d = lax.rem(me + offset, dests)
+        return d, {"row": d // 2, "sub": lax.rem(d, 2)}
+
+    barrier = pltpu.get_barrier_semaphore()
+    pl.semaphore_signal(barrier, inc=1, device_id={"ch": other_ch}, device_id_type=MESH)
+    for offset in range(1, dests):
+        pl.semaphore_signal(barrier, inc=1, device_id=peer(offset)[1], device_id_type=MESH)
+
+    own_rows = pl.ds(pl.multiple_of(ch * HALF, HALF), HALF)
+    local = pltpu.make_async_copy(x_ref, x_all.at[own_rows], local_sem)
+    local.start()
+    pl.semaphore_wait(barrier, dests)
+    x_copies = []
+    for k in range(CHUNKS):
+        cells = pl.ds(k * width, width)
+        copy = pltpu.make_async_remote_copy(
+            src_ref=x_ref.at[:, cells],
+            dst_ref=x_all.at[own_rows, cells],
+            send_sem=x_send.at[k],
+            recv_sem=x_recv.at[k],
+            device_id={"ch": other_ch},
+            device_id_type=MESH,
+        )
+        copy.start()
+        x_copies.append(copy)
+
+    for at, ref in ((0, proj_ref), (256, gate_ref), (512, outgate_ref), (640, out_weight)):
+        turned[at : at + ref.shape[1], :] = jnp.transpose(ref[...].astype(jnp.float32))
+    for slot, base in enumerate((0, 128, 256, 384, 512, 640)):
+        rows_here = pl.ds(pl.multiple_of(base + ch * HALF, HALF), HALF)
+        weights[slot * HALF : (slot + 1) * HALF, :] = turned[rows_here, :].astype(jnp.bfloat16)
+    gain = column(norm_gain[...])
+    shift = column(norm_shift[...])
+    lane = lax.broadcasted_iota(jnp.int32, (16, LANES), 1)
+    low = lane < HALF
+    mask_row = mask_ref[...].astype(jnp.float32)
+    columns[...] = column(mask_row)
+    mask_wide = jnp.broadcast_to(mask_row, (16, LANES))
+    mask_turn = pltpu.roll(mask_wide, HALF, 1)
+    near = jnp.where(low, mask_wide, mask_turn)
+    far = jnp.where(low, mask_turn, mask_wide)
+    second = sub.astype(jnp.float32)
+    col_mask = near * (1.0 - second) + far * second
+    row_at = pl.multiple_of(row * 32, 32)
+    row_mask = jnp.where(low, columns[pl.ds(row_at, 16), :], columns[pl.ds(row_at + 16, 16), :])
+    pair_mask = row_mask * col_mask
+
+    local.wait()
+    gain_wide = spread_gain(gain, width)
+    shift_wide = spread_gain(shift, width)
+    a_copies = []
+    for k in range(CHUNKS):
+        cells = pl.ds(k * width, width)
+        x_copies[k].wait_recv()
+        normed = normalise(x_all[:, cells].astype(jnp.float32), gain_wide, shift_wide)
+        projected = jnp.dot(weights[: 5 * HALF, :], normed, preferred_element_type=jnp.float32)
+        gate_keep[:, cells] = swish_gate(projected[4 * HALF :])
+        both = projected[: 2 * HALF] * swish_gate(projected[2 * HALF : 4 * HALF])
+        for t in range(per):
+            tile = k * per + t
+            block = both[:, t * LANES : (t + 1) * LANES] * pair_mask[tile : tile + 1, :]
+            for d in range(dests):
+                pair = jnp.concatenate(
+                    [block[8 * d : 8 * d + 8], block[HALF + 8 * d : HALF + 8 * d + 8]], axis=0
+                )
+                send_buf[d, tile * 16 : tile * 16 + 16, :] = pair.astype(jnp.bfloat16)
+        span = pl.ds(k * per * 16, per * 16)
+        for offset in range(1, dests):
+            d, where = peer(offset)
+            copy = pltpu.make_async_remote_copy(
+                src_ref=send_buf.at[d, span],
+                dst_ref=recv_buf.at[me, span],
+                send_sem=a_send.at[offset, k],
+                recv_sem=a_recv.at[offset, k],
+                device_id=where,
+                device_id_type=MESH,
+            )
+            copy.start()
+            a_copies.append(copy)
+    recv_buf[me] = send_buf[me]
+    post_gain_wide = spread_gain(column(post_gain[...]), width)
+    post_shift_wide = spread_gain(column(post_shift[...]), width)
+    for copy in a_copies:
+        copy.wait_recv()
+
+    for r in range(rows):
+        for s in range(2):
+            wide[s] = recv_buf[2 * r + s].astype(jnp.float32)
+        for e in range(16):
+            first = wide[0, pl.ds(e, 16, stride=16), :]
+            last = wide[1, pl.ds(e, 16, stride=16), :]
+            top = jnp.where(low, first, pltpu.roll(last, HALF, 1))
+            bottom = jnp.where(low, pltpu.roll(first, HALF, 1), last)
+            panels[e, 32 * r : 32 * r + 16, :] = top.astype(jnp.bfloat16)
+            panels[e, 32 * r + 16 : 32 * r + 32, :] = bottom.astype(jnp.bfloat16)
+
+    for h in range(8):
+        tri = lax.dot_general(
+            panels[h], panels[8 + h], (((1,), (1,)), ((), ())), preferred_element_type=jnp.float32
+        )
+        rolled = pltpu.roll(tri, HALF, 1)
+        for r in range(rows):
+            a, b = slice(32 * r, 32 * r + 16), slice(32 * r + 16, 32 * r + 32)
+            tri_wide[2 * r, pl.ds(h, 16, stride=8), :] = jnp.where(low, tri[a], rolled[b])
+            tri_wide[2 * r + 1, pl.ds(h, 16, stride=8), :] = jnp.where(low, rolled[a], tri[b])
+
+    tri_send[...] = tri_wide[...].astype(jnp.bfloat16)
+    t_copies = []
+    for offset in range(1, dests):
+        d, where = peer(offset)
+        copy = pltpu.make_async_remote_copy(
+            src_ref=tri_send.at[d],
+            dst_ref=tri_all.at[ch, me],
+            send_sem=t_send.at[offset],
+            recv_sem=t_recv.at[offset],
+            device_id=where,
+            device_id_type=MESH,
+        )
+        copy.start()
+        t_copies.append(copy)
+    tri_all[ch, me] = tri_send[me]
+    f_copies = []
+    for offset in range(dests):
+        if offset > 0:
+            t_copies[offset - 1].wait_recv()
+        source = lax.rem(me + dests - offset, dests)
+        copy = pltpu.make_async_remote_copy(
+            src_ref=tri_all.at[ch, source],
+            dst_ref=tri_all.at[ch, source],
+            send_sem=f_send.at[offset],
+            recv_sem=f_recv.at[offset],
+            device_id={"ch": other_ch},
+            device_id_type=MESH,
+        )
+        copy.start()
+        f_copies.append(copy)
+    for copy in f_copies:
+        copy.wait_recv()
+
+    for k in range(CHUNKS):
+        cells = pl.ds(k * width, width)
+        parts = []
+        for t in range(k * per, (k + 1) * per):
+            stack = [
+                tri_all[c, q, t * 8 : t * 8 + 8, :].astype(jnp.float32)
+                for c in range(2)
+                for q in range(dests)
+            ]
+            parts.append(jnp.concatenate(stack, axis=0))
+        post = normalise(jnp.concatenate(parts, axis=1), post_gain_wide, post_shift_wide)
+        update = jnp.dot(weights[5 * HALF :, :], post, preferred_element_type=jnp.float32)
+        o_ref[:, cells] = (update * gate_keep[:, cells]).astype(jnp.bfloat16)
+    for copy in x_copies + a_copies + t_copies + f_copies:
+        copy.wait_send()
+
+
+def fused_body(
+    pair_act,
+    token_mask,
+    norm_gain,
+    norm_shift,
+    proj_weight,
+    gate_weight,
+    outgate_weight,
+    post_gain,
+    post_shift,
+    out_weight,
+):
+    rows = lax.axis_size("row")
+    dests = 2 * rows
+    chan, slab_rows, slab_cols = pair_act.shape
+    cells = slab_rows * slab_cols
+    tiles = cells // LANES
+    flat = pair_act.reshape(chan, 2, tiles, slab_cols).transpose(0, 2, 1, 3).reshape(chan, cells)
+    vmem = pl.BlockSpec(memory_space=pltpu.VMEM)
+    sems = pltpu.SemaphoreType.DMA
+    out = pl.pallas_call(
+        functools.partial(fused_kernel, rows),
+        out_shape=jax.ShapeDtypeStruct((chan, cells), jnp.bfloat16),
+        in_specs=[pl.BlockSpec(memory_space=pl.ANY)] + [vmem] * 9,
+        out_specs=vmem,
+        scratch_shapes=[
+            pltpu.VMEM((2 * chan, cells), jnp.bfloat16),
+            pltpu.VMEM((6 * HALF, LANES), jnp.bfloat16),
+            pltpu.VMEM((768, LANES), jnp.float32),
+            pltpu.VMEM((LANES, LANES), jnp.float32),
+            pltpu.VMEM((chan, cells), jnp.float32),
+            pltpu.VMEM((dests, tiles * 16, LANES), jnp.bfloat16),
+            pltpu.VMEM((dests, tiles * 16, LANES), jnp.bfloat16),
+            pltpu.VMEM((2, tiles * 16, LANES), jnp.float32),
+            pltpu.VMEM((16, LANES, LANES), jnp.bfloat16),
+            pltpu.VMEM((dests, tiles * 8, LANES), jnp.float32),
+            pltpu.VMEM((dests, tiles * 8, LANES), jnp.bfloat16),
+            pltpu.VMEM((2, dests, tiles * 8, LANES), jnp.bfloat16),
+            sems,
+            sems((CHUNKS,)),
+            sems((CHUNKS,)),
+            sems((dests, CHUNKS)),
+            sems((dests, CHUNKS)),
+            sems((dests,)),
+            sems((dests,)),
+            sems((dests,)),
+            sems((dests,)),
+        ],
+        compiler_params=pltpu.CompilerParams(
+            collective_id=0, has_side_effects=True, vmem_limit_bytes=32 * 1024 * 1024
+        ),
+        name="triangle_update",
+    )(
+        flat,
+        token_mask.reshape(1, -1),
+        norm_gain.reshape(1, -1),
+        norm_shift.reshape(1, -1),
+        proj_weight,
+        gate_weight,
+        outgate_weight,
+        post_gain.reshape(1, -1),
+        post_shift.reshape(1, -1),
+        out_weight,
+    )
+    return out.reshape(chan, tiles, 2, slab_cols).transpose(0, 2, 1, 3).reshape(pair_act.shape)
+
+
 def solution(mesh):
     placed = (P("ch", ("grp", "row"), "sub"), P("grp"), P(), P(), P(), P(), P(), P(), P(), P())
-    return jax.shard_map(
-        body, mesh=mesh, in_specs=placed, out_specs=P("ch", ("grp", "row"), "sub"), check_vma=False
-    )
+
+    def update(*arguments):
+        channels, all_rows, tokens = arguments[0].shape
+        hidden = arguments[-1].shape[0]
+        sizes = dict(mesh.shape)
+        fits = (
+            (channels, hidden, tokens) == (128, 128, 128)
+            and (sizes["row"], sizes["ch"], sizes["sub"]) == (4, 2, 2)
+            and all_rows == tokens * sizes["grp"]
+        )
+        return jax.shard_map(
+            fused_body if fits else body,
+            mesh=mesh,
+            in_specs=placed,
+            out_specs=P("ch", ("grp", "row"), "sub"),
+            check_vma=False,
+        )(*arguments)
+
+    return update

time: 137 us -> 38.9 us (0.28)
  waiting for transfers between devices: 52.4 us -> 0 us
  Pallas kernels: 0 us -> 34.9 us
  blocking collectives: 31.1 us -> 0 us
  local copies, waits for them, and re-layouts: 27 us -> 3.65 us
  between operations: 13.6 us -> 0.12 us
  matrix products: 7.58 us -> 0 us
  other arithmetic: 4.8 us -> 0 us
    all_gather x1 -> x0, waiting for transfers between devices: 45 us -> none  [contract(): lax.all_gather(right_panel, 'row', axis=1, tiled=True)]
    pallas_call x0 -> x1, Pallas kernels: none -> 34.9 us  [fused_body(): pl.pallas_call(functools.partial(fused_kernel, rows), out_shape=jax.Shape...]
    all_gather x2 -> x0, blocking collectives: 31.1 us -> none  [the longest x1 15.8 us: body(): gathered = lax.all_gather(pair_act, 'ch', axis=0, tiled=True)]
    unnamed x23 -> x18, local copies, waits for them, and re-layouts: 16.1 us -> 0.36 us
    convert_element_type x4 -> x0, local copies, waits for them, and re-layouts: 9.01 us -> none  [the longest x1 2.54 us: gated_inputs(): left_panel = (projected[:hidden] * jax.nn.sigmoid(projected[2 * hidden:3...]
    unnamed x3 -> x0, waiting for transfers between devices: 7.43 us -> none
    dot_general x2 -> x0, matrix products: 5.97 us -> none  [the longest x1 4.58 us: contract(): jnp.einsum('hik,hjk->hij', left_panel, lax.all_gather(right_panel, 'row',...]
    convert_element_type x4 -> x0, other arithmetic: 3.41 us -> none  [the longest x1 1.86 us: gated_inputs(): right_panel = (projected[hidden:2 * hidden] * jax.nn.sigmoid(projected[3...]
  transfers between devices with their start and end apart: 2 -> 0, of which waited for: 2 -> 0; matrix products, arithmetic and copies ran while one was open for 2% -> 0% of each run, Pallas kernels for 0% -> 0%
where the time goes in v1:
time: 38.9 us; the launch traced here: 38.7 us
  Pallas kernels  34.9 us (90%)
  local copies, waits for them, and re-layouts  3.65 us (9%)
    pallas_call x1, Pallas kernels, fused_body(): pl.pallas_call(functools.partial(fused_kernel, rows), out_shape=jax.Shape...  34.9 us
    reshape x2, local copies, waits for them, and re-layouts, fused_body(): pair_act.reshape(chan, 2, tiles, slab_cols).transpose(0, 2, 1, 3)  1.91 us
    transpose x1, local copies, waits for them, and re-layouts, fused_body(): out.reshape(chan, tiles, 2, slab_cols).transpose(0, 2, 1, 3)  0.87 us

profile of v1, /device:TPU:0, one launch (start us, length us, event | category | flops | bytes accessed | tf_op | source)
XLA Modules:
  0.0 38.7 jit_solution(4234380765714571233)
XLA Ops:
  0.0 1.5 %copy.14 = bf16[64,2,16,64]{3,1,2,0:T(2,128)(2,1)S(1)} copy(bf16[64,2,16,64]{3,2,1,0:T(8,128)(2,1)} %bitcast.18) | data formatting | bytes 524288 | tf_op jit(solution)/shard_map/reshape | solution.py:340
  1.5 0.0 copy-start
  1.5 0.0 copy-start.1
  1.5 0.0 copy-start.2
  1.5 0.0 copy-start.3
  1.5 0.0 copy-start.4
  1.5 0.0 copy-start.5
  1.5 0.0 copy-start.6
  1.5 0.0 copy-start.7
  1.6 0.0 copy-start.8
  1.6 0.5 %reshape.28.x_ref = bf16[64,2048]{1,0:T(8,128)(2,1)S(1)} reshape(bf16[64,16,2,64]{3,2,1,0:T(2,128)(2,1)S(1)} %bitcast.17) | data formatting | bytes 524288 | tf_op jit(solution)/shard_map/reshape | solution.py:340
  2.0 0.3 copy-done
  2.3 0.0 copy-done.1
  2.3 0.0 copy-done.2
  2.3 0.0 copy-done.3
  2.3 0.0 copy-done.4
  2.3 0.0 copy-done.5
  2.3 0.0 copy-done.6
  2.4 0.0 copy-done.7
  2.4 0.0 copy-done.8
  2.4 34.9 %triangle_update.1 = bf16[64,2048]{1,0:T(8,128)(2,1)S(1)} custom-call(bf16[64,2048]{1,0:T(8,128)(2,1)S(1)} %reshape.28.x_ref, s32[1,128]{1,0:T(1,128)S(1)} %bitcast.11, f32[1,128]{1,0:T(1,128)S(1)} %bitcast.12, f32[1,128]{1,0:T(1,128)S(1)} %bitcast.13, bf16[128,256]{1,0:T(8,128)(2,1)S(1)} %copy-done, bf16[128,256]{1,0:T(8,128)(2,1)S(1)} %copy-done.1, ...), custom_call_target="tpu_custom_call" | custom-call | tf_op jit(solution)/shard_map/triangle_update/pallas_call | solution.py:343
  37.3 0.5 %reshape.34 = bf16[64,16,2,64]{3,2,1,0:T(2,128)(2,1)S(1)} reshape(bf16[64,2048]{1,0:T(8,128)(2,1)S(1)} %triangle_update.1) | data formatting | bytes 524288 | tf_op jit(solution)/shard_map/reshape | solution.py:387
  37.8 0.9 %copy.12 = bf16[64,2,16,64]{3,2,1,0:T(8,128)(2,1)} copy(bf16[64,2,16,64]{3,1,2,0:T(2,128)(2,1)S(1)} %bitcast.16) | data formatting | bytes 524288 | tf_op jit(solution)/shard_map/transpose | solution.py:387
Async XLA Ops:
  1.5 0.8 %copy-start = (bf16[128,256]{1,0:T(8,128)(2,1)S(1)}, bf16[128,256]{1,0:T(8,128)(2,1)}, u32[]{:S(2)}) copy-start(bf16[128,256]{1,0:T(8,128)(2,1)} %proj_ref.1) | copy-start | bytes 196612
  1.5 0.9 %copy-start.1 = (bf16[128,256]{1,0:T(8,128)(2,1)S(1)}, bf16[128,256]{1,0:T(8,128)(2,1)}, u32[]{:S(2)}) copy-start(bf16[128,256]{1,0:T(8,128)(2,1)} %gate_ref.1) | copy-start | bytes 196612
  1.5 0.9 %copy-start.2 = (bf16[128,128]{1,0:T(8,128)(2,1)S(1)}, bf16[128,128]{1,0:T(8,128)(2,1)}, u32[]{:S(2)}) copy-start(bf16[128,128]{1,0:T(8,128)(2,1)} %outgate_ref.1) | copy-start | bytes 98308
  1.5 0.8 %copy-start.3 = (bf16[128,128]{1,0:T(8,128)(2,1)S(1)}, bf16[128,128]{1,0:T(8,128)(2,1)}, u32[]{:S(2)}) copy-start(bf16[128,128]{1,0:T(8,128)(2,1)} %out_weight.1) | copy-start | bytes 98308
  1.5 0.8 %copy-start.4 = (s32[128]{0:T(128)S(1)}, s32[128]{0:T(128)}, u32[]{:S(2)}) copy-start(s32[128]{0:T(128)} %param.11) | copy-start | bytes 1540
  1.5 0.8 %copy-start.5 = (f32[128]{0:T(128)S(1)}, f32[128]{0:T(128)}, u32[]{:S(2)}) copy-start(f32[128]{0:T(128)} %param.12) | copy-start | bytes 1540
  1.5 0.8 %copy-start.6 = (f32[128]{0:T(128)S(1)}, f32[128]{0:T(128)}, u32[]{:S(2)}) copy-start(f32[128]{0:T(128)} %param.13) | copy-start | bytes 1540
  1.5 0.8 %copy-start.7 = (f32[128]{0:T(128)S(1)}, f32[128]{0:T(128)}, u32[]{:S(2)}) copy-start(f32[128]{0:T(128)} %param.17) | copy-start | bytes 1540
  1.6 0.8 %copy-start.8 = (f32[128]{0:T(128)S(1)}, f32[128]{0:T(128)}, u32[]{:S(2)}) copy-start(f32[128]{0:T(128)} %param.18) | copy-start | bytes 1540

commit v2 on v1

--- a/solution.py
+++ b/solution.py
@@ -134,12 +134,14 @@
     x_all,
     weights,
     turned,
+    wide_weights,
     columns,
     gate_keep,
     send_buf,
     recv_buf,
     wide,
     panels,
+    natural,
     tri_wide,
     tri_send,
     tri_all,
@@ -163,14 +165,17 @@
     per = tiles // CHUNKS
     width = per * LANES
 
-    def peer(offset):
-        d = lax.rem(me + offset, dests)
-        return d, {"row": d // 2, "sub": lax.rem(d, 2)}
+    near = row + 1 - 2 * lax.rem(row, 2)
+    peers = []
+    for there in (lax.rem(row + 2, rows), rows - 1 - row, near, row):
+        for core in (sub, 1 - sub):
+            peers.append((there * 2 + core, {"row": there, "sub": core}))
+    peers = peers[:6] + peers[7:]
 
     barrier = pltpu.get_barrier_semaphore()
     pl.semaphore_signal(barrier, inc=1, device_id={"ch": other_ch}, device_id_type=MESH)
-    for offset in range(1, dests):
-        pl.semaphore_signal(barrier, inc=1, device_id=peer(offset)[1], device_id_type=MESH)
+    for _, where in peers:
+        pl.semaphore_signal(barrier, inc=1, device_id=where, device_id_type=MESH)
 
     own_rows = pl.ds(pl.multiple_of(ch * HALF, HALF), HALF)
     local = pltpu.make_async_copy(x_ref, x_all.at[own_rows], local_sem)
@@ -192,7 +197,19 @@
 
     for at, ref in ((0, proj_ref), (256, gate_ref), (512, outgate_ref), (640, out_weight)):
         turned[at : at + ref.shape[1], :] = jnp.transpose(ref[...].astype(jnp.float32))
-    for slot, base in enumerate((0, 128, 256, 384, 512, 640)):
+    sublane = lax.broadcasted_iota(jnp.int32, (8, LANES), 0)
+    upper = sublane < 4
+    for slot, base in ((0, 0), (1, 256)):
+        for m in range(dests):
+            at = pl.multiple_of(base + ch * HALF, HALF) + 8 * m
+            left = turned[pl.ds(at, 8), :]
+            right = turned[pl.ds(at + 128, 8), :]
+            first = jnp.where(upper, left, pltpu.roll(right, 4, 0))
+            last = jnp.where(upper, pltpu.roll(left, 4, 0), right)
+            wide_weights[128 * slot + 8 * m : 128 * slot + 8 * m + 8, :] = first
+            wide_weights[128 * slot + HALF + 8 * m : 128 * slot + HALF + 8 * m + 8, :] = last
+    weights[:256, :] = wide_weights[...].astype(jnp.bfloat16)
+    for slot, base in ((4, 512), (5, 640)):
         rows_here = pl.ds(pl.multiple_of(base + ch * HALF, HALF), HALF)
         weights[slot * HALF : (slot + 1) * HALF, :] = turned[rows_here, :].astype(jnp.bfloat16)
     gain = column(norm_gain[...])
@@ -203,18 +220,35 @@
     columns[...] = column(mask_row)
     mask_wide = jnp.broadcast_to(mask_row, (16, LANES))
     mask_turn = pltpu.roll(mask_wide, HALF, 1)
-    near = jnp.where(low, mask_wide, mask_turn)
-    far = jnp.where(low, mask_turn, mask_wide)
+    inner = jnp.where(low, mask_wide, mask_turn)
+    outer = jnp.where(low, mask_turn, mask_wide)
     second = sub.astype(jnp.float32)
-    col_mask = near * (1.0 - second) + far * second
+    col_mask = inner * (1.0 - second) + outer * second
     row_at = pl.multiple_of(row * 32, 32)
-    row_mask = jnp.where(low, columns[pl.ds(row_at, 16), :], columns[pl.ds(row_at + 16, 16), :])
+    even = columns[pl.ds(row_at, 16, stride=2), :]
+    odd = columns[pl.ds(row_at + 1, 16, stride=2), :]
+    row_mask = jnp.where(low, even, odd)
     pair_mask = row_mask * col_mask
 
     local.wait()
     gain_wide = spread_gain(gain, width)
     shift_wide = spread_gain(shift, width)
-    a_copies = []
+    a_copies = [[], []]
+
+    def send_panels(part, piece, first, count):
+        span = pl.ds(first * 8, count * 8)
+        for p, (d, where) in enumerate(peers):
+            copy = pltpu.make_async_remote_copy(
+                src_ref=send_buf.at[part, d, span],
+                dst_ref=recv_buf.at[part, me, span],
+                send_sem=a_send.at[part, p, piece],
+                recv_sem=a_recv.at[part, p, piece],
+                device_id=where,
+                device_id_type=MESH,
+            )
+            copy.start()
+            a_copies[part].append(copy)
+
     for k in range(CHUNKS):
         cells = pl.ds(k * width, width)
         x_copies[k].wait_recv()
@@ -222,101 +256,114 @@
         projected = jnp.dot(weights[: 5 * HALF, :], normed, preferred_element_type=jnp.float32)
         gate_keep[:, cells] = swish_gate(projected[4 * HALF :])
         both = projected[: 2 * HALF] * swish_gate(projected[2 * HALF : 4 * HALF])
-        for t in range(per):
+        for t in range(0, per, 2):
             tile = k * per + t
-            block = both[:, t * LANES : (t + 1) * LANES] * pair_mask[tile : tile + 1, :]
-            for d in range(dests):
-                pair = jnp.concatenate(
-                    [block[8 * d : 8 * d + 8], block[HALF + 8 * d : HALF + 8 * d + 8]], axis=0
-                )
-                send_buf[d, tile * 16 : tile * 16 + 16, :] = pair.astype(jnp.bfloat16)
-        span = pl.ds(k * per * 16, per * 16)
-        for offset in range(1, dests):
-            d, where = peer(offset)
+            one = both[:, t * LANES : (t + 1) * LANES] * pair_mask[tile : tile + 1, :]
+            two = both[:, (t + 1) * LANES : (t + 2) * LANES] * pair_mask[tile + 1 : tile + 2, :]
+            for part in range(2):
+                for d in range(dests):
+                    at = HALF * part + 8 * d
+                    pair = jnp.concatenate([one[at : at + 8], two[at : at + 8]], axis=0)
+                    send_buf[part, d, tile * 8 : tile * 8 + 16, :] = pair.astype(jnp.bfloat16)
+        send_panels(0, k, k * per, per)
+        if k == 0:
+            send_panels(1, 0, 0, per)
+    send_panels(1, 1, per, tiles - per)
+    for part in range(2):
+        recv_buf[part, me] = send_buf[part, me]
+    post_gain_wide = spread_gain(column(post_gain[...]), width)
+    post_shift_wide = spread_gain(column(post_shift[...]), width)
+
+    def products(part):
+        for copy in a_copies[part]:
+            copy.wait_recv()
+        for r in range(rows):
+            for s in range(2):
+                wide[s] = recv_buf[part, 2 * r + s].astype(jnp.float32)
+            for e in range(8):
+                first = wide[0, pl.ds(e, 16, stride=8), :]
+                last = wide[1, pl.ds(e, 16, stride=8), :]
+                top = jnp.where(low, first, pltpu.roll(last, HALF, 1))
+                bottom = jnp.where(low, pltpu.roll(first, HALF, 1), last)
+                if e < 4:
+                    panels[part, e, 32 * r : 32 * r + 16, :] = top.astype(jnp.bfloat16)
+                    panels[part, e, 32 * r + 16 : 32 * r + 32, :] = bottom.astype(jnp.bfloat16)
+                else:
+                    natural[e - 4, pl.ds(32 * r, 16, stride=2), :] = top
+                    natural[e - 4, pl.ds(32 * r + 1, 16, stride=2), :] = bottom
+        for h in range(4):
+            tri = lax.dot_general(
+                panels[part, h],
+                natural[h].astype(jnp.bfloat16),
+                (((1,), (1,)), ((), ())),
+                preferred_element_type=jnp.float32,
+            )
+            rolled = pltpu.roll(tri, HALF, 1)
+            for r in range(rows):
+                a, b = slice(32 * r, 32 * r + 16), slice(32 * r + 16, 32 * r + 32)
+                tri_wide[2 * r, pl.ds(h, 16, stride=4), :] = jnp.where(low, tri[a], rolled[b])
+                tri_wide[2 * r + 1, pl.ds(h, 16, stride=4), :] = jnp.where(low, rolled[a], tri[b])
+        tri_send[part] = tri_wide[...].astype(jnp.bfloat16)
+
+    t_copies = [[], []]
+    f_copies = []
+
+    def send_products(part):
+        for p, (d, where) in enumerate(peers):
             copy = pltpu.make_async_remote_copy(
-                src_ref=send_buf.at[d, span],
-                dst_ref=recv_buf.at[me, span],
-                send_sem=a_send.at[offset, k],
-                recv_sem=a_recv.at[offset, k],
+                src_ref=tri_send.at[part, d],
+                dst_ref=tri_all.at[ch, part, me],
+                send_sem=t_send.at[part, p],
+                recv_sem=t_recv.at[part, p],
                 device_id=where,
                 device_id_type=MESH,
             )
             copy.start()
-            a_copies.append(copy)
-    recv_buf[me] = send_buf[me]
-    post_gain_wide = spread_gain(column(post_gain[...]), width)
-    post_shift_wide = spread_gain(column(post_shift[...]), width)
-    for copy in a_copies:
-        copy.wait_recv()
-
-    for r in range(rows):
-        for s in range(2):
-            wide[s] = recv_buf[2 * r + s].astype(jnp.float32)
-        for e in range(16):
-            first = wide[0, pl.ds(e, 16, stride=16), :]
-            last = wide[1, pl.ds(e, 16, stride=16), :]
-            top = jnp.where(low, first, pltpu.roll(last, HALF, 1))
-            bottom = jnp.where(low, pltpu.roll(first, HALF, 1), last)
-            panels[e, 32 * r : 32 * r + 16, :] = top.astype(jnp.bfloat16)
-            panels[e, 32 * r + 16 : 32 * r + 32, :] = bottom.astype(jnp.bfloat16)
-
-    for h in range(8):
-        tri = lax.dot_general(
-            panels[h], panels[8 + h], (((1,), (1,)), ((), ())), preferred_element_type=jnp.float32
-        )
-        rolled = pltpu.roll(tri, HALF, 1)
-        for r in range(rows):
-            a, b = slice(32 * r, 32 * r + 16), slice(32 * r + 16, 32 * r + 32)
-            tri_wide[2 * r, pl.ds(h, 16, stride=8), :] = jnp.where(low, tri[a], rolled[b])
-            tri_wide[2 * r + 1, pl.ds(h, 16, stride=8), :] = jnp.where(low, rolled[a], tri[b])
-
-    tri_send[...] = tri_wide[...].astype(jnp.bfloat16)
-    t_copies = []
-    for offset in range(1, dests):
-        d, where = peer(offset)
-        copy = pltpu.make_async_remote_copy(
-            src_ref=tri_send.at[d],
-            dst_ref=tri_all.at[ch, me],
-            send_sem=t_send.at[offset],
-            recv_sem=t_recv.at[offset],
-            device_id=where,
-            device_id_type=MESH,
-        )
-        copy.start()
-        t_copies.append(copy)
-    tri_all[ch, me] = tri_send[me]
-    f_copies = []
-    for offset in range(dests):
-        if offset > 0:
-            t_copies[offset - 1].wait_recv()
-        source = lax.rem(me + dests - offset, dests)
-        copy = pltpu.make_async_remote_copy(
-            src_ref=tri_all.at[ch, source],
-            dst_ref=tri_all.at[ch, source],
-            send_sem=f_send.at[offset],
-            recv_sem=f_recv.at[offset],
-            device_id={"ch": other_ch},
-            device_id_type=MESH,
-        )
-        copy.start()
-        f_copies.append(copy)
+            t_copies[part].append(copy)
+        tri_all[ch, part, me] = tri_send[part, me]
+
+    def forward(part):
+        sources = [me] + [d for d, _ in peers]
+        for p, source in enumerate(sources):
+            if p > 0:
+                t_copies[part][p - 1].wait_recv()
+            copy = pltpu.make_async_remote_copy(
+                src_ref=tri_all.at[ch, part, source],
+                dst_ref=tri_all.at[ch, part, source],
+                send_sem=f_send.at[part, p],
+                recv_sem=f_recv.at[part, p],
+                device_id={"ch": other_ch},
+                device_id_type=MESH,
+            )
+            copy.start()
+            f_copies.append(copy)
+
+    products(0)
+    send_products(0)
+    products(1)
+    send_products(1)
+    forward(0)
+    forward(1)
     for copy in f_copies:
         copy.wait_recv()
 
     for k in range(CHUNKS):
         cells = pl.ds(k * width, width)
         parts = []
-        for t in range(k * per, (k + 1) * per):
-            stack = [
-                tri_all[c, q, t * 8 : t * 8 + 8, :].astype(jnp.float32)
-                for c in range(2)
-                for q in range(dests)
-            ]
-            parts.append(jnp.concatenate(stack, axis=0))
+        for t in range(k * per, (k + 1) * per, 2):
+            evens, odds = [], []
+            for c in range(2):
+                for q in range(dests):
+                    one = tri_all[c, 0, q, t * 4 : t * 4 + 8, :].astype(jnp.float32)
+                    two = tri_all[c, 1, q, t * 4 : t * 4 + 8, :].astype(jnp.float32)
+                    evens.append(jnp.where(upper, one, pltpu.roll(two, 4, 0)))
+                    odds.append(jnp.where(upper, pltpu.roll(one, 4, 0), two))
+            parts.append(jnp.concatenate(evens, axis=0))
+            parts.append(jnp.concatenate(odds, axis=0))
         post = normalise(jnp.concatenate(parts, axis=1), post_gain_wide, post_shift_wide)
         update = jnp.dot(weights[5 * HALF :, :], post, preferred_element_type=jnp.float32)
         o_ref[:, cells] = (update * gate_keep[:, cells]).astype(jnp.bfloat16)
-    for copy in x_copies + a_copies + t_copies + f_copies:
+    for copy in x_copies + a_copies[0] + a_copies[1] + t_copies[0] + t_copies[1] + f_copies:
         copy.wait_send()
 
 
@@ -337,7 +384,7 @@
     chan, slab_rows, slab_cols = pair_act.shape
     cells = slab_rows * slab_cols
     tiles = cells // LANES
-    flat = pair_act.reshape(chan, 2, tiles, slab_cols).transpose(0, 2, 1, 3).reshape(chan, cells)
+    flat = pair_act.reshape(chan, cells)
     vmem = pl.BlockSpec(memory_space=pltpu.VMEM)
     sems = pltpu.SemaphoreType.DMA
     out = pl.pallas_call(
@@ -349,24 +396,26 @@
             pltpu.VMEM((2 * chan, cells), jnp.bfloat16),
             pltpu.VMEM((6 * HALF, LANES), jnp.bfloat16),
             pltpu.VMEM((768, LANES), jnp.float32),
+            pltpu.VMEM((4 * HALF, LANES), jnp.float32),
             pltpu.VMEM((LANES, LANES), jnp.float32),
             pltpu.VMEM((chan, cells), jnp.float32),
-            pltpu.VMEM((dests, tiles * 16, LANES), jnp.bfloat16),
-            pltpu.VMEM((dests, tiles * 16, LANES), jnp.bfloat16),
-            pltpu.VMEM((2, tiles * 16, LANES), jnp.float32),
-            pltpu.VMEM((16, LANES, LANES), jnp.bfloat16),
-            pltpu.VMEM((dests, tiles * 8, LANES), jnp.float32),
-            pltpu.VMEM((dests, tiles * 8, LANES), jnp.bfloat16),
             pltpu.VMEM((2, dests, tiles * 8, LANES), jnp.bfloat16),
+            pltpu.VMEM((2, dests, tiles * 8, LANES), jnp.bfloat16),
+            pltpu.VMEM((2, tiles * 8, LANES), jnp.float32),
+            pltpu.VMEM((2, 4, LANES, LANES), jnp.bfloat16),
+            pltpu.VMEM((4, LANES, LANES), jnp.float32),
+            pltpu.VMEM((dests, tiles * 4, LANES), jnp.float32),
+            pltpu.VMEM((2, dests, tiles * 4, LANES), jnp.bfloat16),
+            pltpu.VMEM((2, 2, dests, tiles * 4, LANES), jnp.bfloat16),
             sems,
             sems((CHUNKS,)),
             sems((CHUNKS,)),
-            sems((dests, CHUNKS)),
-            sems((dests, CHUNKS)),
-            sems((dests,)),
-            sems((dests,)),
-            sems((dests,)),
-            sems((dests,)),
+            sems((2, dests, CHUNKS)),
+            sems((2, dests, CHUNKS)),
+            sems((2, dests)),
+            sems((2, dests)),
+            sems((2, dests)),
+            sems((2, dests)),
         ],
         compiler_params=pltpu.CompilerParams(
             collective_id=0, has_side_effects=True, vmem_limit_bytes=32 * 1024 * 1024
@@ -384,7 +433,7 @@
         post_shift.reshape(1, -1),
         out_weight,
     )
-    return out.reshape(chan, tiles, 2, slab_cols).transpose(0, 2, 1, 3).reshape(pair_act.shape)
+    return out.reshape(pair_act.shape)
 
 
 def solution(mesh):

time: 38.9 us -> 38.2 us (0.982)
  local copies, waits for them, and re-layouts: 3.65 us -> 2.96 us
    transpose x1 -> x0, local copies, waits for them, and re-layouts: 0.87 us -> none  [fused_body(): out.reshape(chan, tiles, 2, slab_cols).transpose(0, 2, 1, 3)]
    reshape x3 -> x2, local copies, waits for them, and re-layouts: 2.43 us -> 2.92 us  [the longest x1 1.61 us: fused_body(): flat = pair_act.reshape(chan, cells)]
where the time goes in v2:
time: 38.2 us; the launch traced here: 38.1 us
  Pallas kernels  35 us (92%)
  local copies, waits for them, and re-layouts  2.96 us (8%)
    pallas_call x1, Pallas kernels, fused_body(): pl.pallas_call(functools.partial(fused_kernel, rows), out_shape=jax.Shape...  35 us
    reshape x1, local copies, waits for them, and re-layouts, fused_body(): flat = pair_act.reshape(chan, cells)  1.61 us
    reshape x1, local copies, waits for them, and re-layouts, fused_body(): return out.reshape(pair_act.shape)  1.31 us

profile of v2, /device:TPU:0, one launch (start us, length us, event | category | flops | bytes accessed | tf_op | source)
XLA Modules:
  0.0 38.1 jit_solution(17765357964576274828)
XLA Ops:
  0.0 0.0 copy-start
  0.0 0.0 copy-start.1
  0.0 0.0 copy-start.2
  0.0 0.0 copy-start.3
  0.0 0.0 copy-start.4
  0.0 0.0 copy-start.5
  0.0 0.0 copy-start.6
  0.0 0.0 copy-start.7
  0.0 0.0 copy-start.8
  0.1 1.6 %reshape.21.x_ref = bf16[64,2048]{1,0:T(8,128)(2,1)S(1)} reshape(bf16[64,32,64]{2,1,0:T(8,128)(2,1)} %param.10) | data formatting | bytes 524288 | tf_op jit(solution)/shard_map/reshape | solution.py:387
  1.7 0.0 copy-done
  1.7 0.0 copy-done.1
  1.7 0.0 copy-done.2
  1.7 0.0 copy-done.3
  1.7 0.0 copy-done.4
  1.7 0.0 copy-done.5
  1.7 0.0 copy-done.6
  1.7 0.0 copy-done.7
  1.7 0.0 copy-done.8
  1.8 35.0 %triangle_update.1 = bf16[64,2048]{1,0:T(8,128)(2,1)S(1)} custom-call(bf16[64,2048]{1,0:T(8,128)(2,1)S(1)} %reshape.21.x_ref, s32[1,128]{1,0:T(1,128)S(1)} %bitcast.5, f32[1,128]{1,0:T(1,128)S(1)} %bitcast.6, f32[1,128]{1,0:T(1,128)S(1)} %bitcast.7, bf16[128,256]{1,0:T(8,128)(2,1)S(1)} %copy-done, bf16[128,256]{1,0:T(8,128)(2,1)S(1)} %copy-done.1, ...), custom_call_target="tpu_custom_call" | custom-call | tf_op jit(solution)/shard_map/triangle_update/pallas_call | solution.py:390
  36.8 1.3 %reshape.27 = bf16[64,32,64]{2,1,0:T(8,128)(2,1)} reshape(bf16[64,2048]{1,0:T(8,128)(2,1)S(1)} %triangle_update.1) | data formatting | bytes 524288 | tf_op jit(solution)/shard_map/reshape | solution.py:436
Async XLA Ops:
  0.0 1.7 %copy-start = (bf16[128,256]{1,0:T(8,128)(2,1)S(1)}, bf16[128,256]{1,0:T(8,128)(2,1)}, u32[]{:S(2)}) copy-start(bf16[128,256]{1,0:T(8,128)(2,1)} %proj_ref.1) | copy-start | bytes 196612
  0.0 1.7 %copy-start.1 = (bf16[128,256]{1,0:T(8,128)(2,1)S(1)}, bf16[128,256]{1,0:T(8,128)(2,1)}, u32[]{:S(2)}) copy-start(bf16[128,256]{1,0:T(8,128)(2,1)} %gate_ref.1) | copy-start | bytes 196612
  0.0 1.7 %copy-start.2 = (bf16[128,128]{1,0:T(8,128)(2,1)S(1)}, bf16[128,128]{1,0:T(8,128)(2,1)}, u32[]{:S(2)}) copy-start(bf16[128,128]{1,0:T(8,128)(2,1)} %outgate_ref.1) | copy-start | bytes 98308
  0.0 1.7 %copy-start.3 = (bf16[128,128]{1,0:T(8,128)(2,1)S(1)}, bf16[128,128]{1,0:T(8,128)(2,1)}, u32[]{:S(2)}) copy-start(bf16[128,128]{1,0:T(8,128)(2,1)} %out_weight.1) | copy-start | bytes 98308
  0.0 1.7 %copy-start.4 = (s32[128]{0:T(128)S(1)}, s32[128]{0:T(128)}, u32[]{:S(2)}) copy-start(s32[128]{0:T(128)} %param.11) | copy-start | bytes 1540
  0.0 1.7 %copy-start.5 = (f32[128]{0:T(128)S(1)}, f32[128]{0:T(128)}, u32[]{:S(2)}) copy-start(f32[128]{0:T(128)} %param.12) | copy-start | bytes 1540
  0.0 1.7 %copy-start.6 = (f32[128]{0:T(128)S(1)}, f32[128]{0:T(128)}, u32[]{:S(2)}) copy-start(f32[128]{0:T(128)} %param.13) | copy-start | bytes 1540
  0.0 1.7 %copy-start.7 = (f32[128]{0:T(128)S(1)}, f32[128]{0:T(128)}, u32[]{:S(2)}) copy-start(f32[128]{0:T(128)} %param.17) | copy-start | bytes 1540
  0.0 1.7 %copy-start.8 = (f32[128]{0:T(128)S(1)}, f32[128]{0:T(128)}, u32[]{:S(2)}) copy-start(f32[128]{0:T(128)} %param.18) | copy-start | bytes 1540

commit v3 on v2

--- a/solution.py
+++ b/solution.py
@@ -134,7 +134,6 @@
     x_all,
     weights,
     turned,
-    wide_weights,
     columns,
     gate_keep,
     send_buf,
@@ -167,10 +166,10 @@
 
     near = row + 1 - 2 * lax.rem(row, 2)
     peers = []
-    for there in (lax.rem(row + 2, rows), rows - 1 - row, near, row):
+    for there in (row, near, lax.rem(row + 2, rows), rows - 1 - row):
         for core in (sub, 1 - sub):
             peers.append((there * 2 + core, {"row": there, "sub": core}))
-    peers = peers[:6] + peers[7:]
+    peers = peers[1:]
 
     barrier = pltpu.get_barrier_semaphore()
     pl.semaphore_signal(barrier, inc=1, device_id={"ch": other_ch}, device_id_type=MESH)
@@ -197,19 +196,7 @@
 
     for at, ref in ((0, proj_ref), (256, gate_ref), (512, outgate_ref), (640, out_weight)):
         turned[at : at + ref.shape[1], :] = jnp.transpose(ref[...].astype(jnp.float32))
-    sublane = lax.broadcasted_iota(jnp.int32, (8, LANES), 0)
-    upper = sublane < 4
-    for slot, base in ((0, 0), (1, 256)):
-        for m in range(dests):
-            at = pl.multiple_of(base + ch * HALF, HALF) + 8 * m
-            left = turned[pl.ds(at, 8), :]
-            right = turned[pl.ds(at + 128, 8), :]
-            first = jnp.where(upper, left, pltpu.roll(right, 4, 0))
-            last = jnp.where(upper, pltpu.roll(left, 4, 0), right)
-            wide_weights[128 * slot + 8 * m : 128 * slot + 8 * m + 8, :] = first
-            wide_weights[128 * slot + HALF + 8 * m : 128 * slot + HALF + 8 * m + 8, :] = last
-    weights[:256, :] = wide_weights[...].astype(jnp.bfloat16)
-    for slot, base in ((4, 512), (5, 640)):
+    for slot, base in enumerate((128, 0, 384, 256, 512, 640)):
         rows_here = pl.ds(pl.multiple_of(base + ch * HALF, HALF), HALF)
         weights[slot * HALF : (slot + 1) * HALF, :] = turned[rows_here, :].astype(jnp.bfloat16)
     gain = column(norm_gain[...])
@@ -268,102 +255,117 @@
         send_panels(0, k, k * per, per)
         if k == 0:
             send_panels(1, 0, 0, per)
-    send_panels(1, 1, per, tiles - per)
+    for k in range(1, CHUNKS):
+        send_panels(1, k, k * per, per)
     for part in range(2):
         recv_buf[part, me] = send_buf[part, me]
     post_gain_wide = spread_gain(column(post_gain[...]), width)
     post_shift_wide = spread_gain(column(post_shift[...]), width)
 
-    def products(part):
-        for copy in a_copies[part]:
-            copy.wait_recv()
+    for copy in a_copies[0]:
+        copy.wait_recv()
+    for r in range(rows):
+        for s in range(2):
+            wide[s, : tiles * 8, :] = recv_buf[0, 2 * r + s].astype(jnp.float32)
+        for e in range(8):
+            first = wide[0, pl.ds(e, 16, stride=8), :]
+            last = wide[1, pl.ds(e, 16, stride=8), :]
+            even = jnp.where(low, first, pltpu.roll(last, HALF, 1))
+            odd = jnp.where(low, pltpu.roll(first, HALF, 1), last)
+            natural[e, pl.ds(32 * r, 16, stride=2), :] = even
+            natural[e, pl.ds(32 * r + 1, 16, stride=2), :] = odd
+    panels[...] = natural[...].astype(jnp.bfloat16)
+
+    block_rows = per * 8
+    count = rows * per
+    wide_low = lax.broadcasted_iota(jnp.int32, (count, LANES), 1) < HALF
+    t_copies, f_copies = [], []
+
+    def products(k):
+        for p in range(dests - 1):
+            a_copies[1][k * (dests - 1) + p].wait_recv()
         for r in range(rows):
             for s in range(2):
-                wide[s] = recv_buf[part, 2 * r + s].astype(jnp.float32)
-            for e in range(8):
-                first = wide[0, pl.ds(e, 16, stride=8), :]
-                last = wide[1, pl.ds(e, 16, stride=8), :]
-                top = jnp.where(low, first, pltpu.roll(last, HALF, 1))
-                bottom = jnp.where(low, pltpu.roll(first, HALF, 1), last)
-                if e < 4:
-                    panels[part, e, 32 * r : 32 * r + 16, :] = top.astype(jnp.bfloat16)
-                    panels[part, e, 32 * r + 16 : 32 * r + 32, :] = bottom.astype(jnp.bfloat16)
-                else:
-                    natural[e - 4, pl.ds(32 * r, 16, stride=2), :] = top
-                    natural[e - 4, pl.ds(32 * r + 1, 16, stride=2), :] = bottom
-        for h in range(4):
+                part = recv_buf[1, 2 * r + s, k * block_rows : (k + 1) * block_rows, :]
+                wide[s, r * block_rows : (r + 1) * block_rows, :] = part.astype(jnp.float32)
+        for e in range(8):
+            first = wide[0, pl.ds(e, count, stride=8), :]
+            last = wide[1, pl.ds(e, count, stride=8), :]
+            even = jnp.where(wide_low, first, pltpu.roll(last, HALF, 1))
+            odd = jnp.where(wide_low, pltpu.roll(first, HALF, 1), last)
+            left = jnp.concatenate([even, odd], axis=0).astype(jnp.bfloat16)
             tri = lax.dot_general(
-                panels[part, h],
-                natural[h].astype(jnp.bfloat16),
-                (((1,), (1,)), ((), ())),
-                preferred_element_type=jnp.float32,
+                left, panels[e], (((1,), (1,)), ((), ())), preferred_element_type=jnp.float32
             )
             rolled = pltpu.roll(tri, HALF, 1)
-            for r in range(rows):
-                a, b = slice(32 * r, 32 * r + 16), slice(32 * r + 16, 32 * r + 32)
-                tri_wide[2 * r, pl.ds(h, 16, stride=4), :] = jnp.where(low, tri[a], rolled[b])
-                tri_wide[2 * r + 1, pl.ds(h, 16, stride=4), :] = jnp.where(low, rolled[a], tri[b])
-        tri_send[part] = tri_wide[...].astype(jnp.bfloat16)
-
-    t_copies = [[], []]
-    f_copies = []
-
-    def send_products(part):
+            tri_wide[0, pl.ds(e, count, stride=8), :] = jnp.where(
+                wide_low, tri[:count], rolled[count:]
+            )
+            tri_wide[1, pl.ds(e, count, stride=8), :] = jnp.where(
+                wide_low, rolled[:count], tri[count:]
+            )
+        for r in range(rows):
+            for s in range(2):
+                part = tri_wide[s, r * block_rows : (r + 1) * block_rows, :]
+                tri_send[k, 2 * r + s] = part.astype(jnp.bfloat16)
         for p, (d, where) in enumerate(peers):
             copy = pltpu.make_async_remote_copy(
-                src_ref=tri_send.at[part, d],
-                dst_ref=tri_all.at[ch, part, me],
-                send_sem=t_send.at[part, p],
-                recv_sem=t_recv.at[part, p],
+                src_ref=tri_send.at[k, d],
+                dst_ref=tri_all.at[ch, k, me],
+                send_sem=t_send.at[k, p],
+                recv_sem=t_recv.at[k, p],
                 device_id=where,
                 device_id_type=MESH,
             )
             copy.start()
-            t_copies[part].append(copy)
-        tri_all[ch, part, me] = tri_send[part, me]
-
-    def forward(part):
-        sources = [me] + [d for d, _ in peers]
-        for p, source in enumerate(sources):
-            if p > 0:
-                t_copies[part][p - 1].wait_recv()
-            copy = pltpu.make_async_remote_copy(
-                src_ref=tri_all.at[ch, part, source],
-                dst_ref=tri_all.at[ch, part, source],
-                send_sem=f_send.at[part, p],
-                recv_sem=f_recv.at[part, p],
-                device_id={"ch": other_ch},
-                device_id_type=MESH,
-            )
-            copy.start()
-            f_copies.append(copy)
-
-    products(0)
-    send_products(0)
-    products(1)
-    send_products(1)
-    forward(0)
-    forward(1)
-    for copy in f_copies:
-        copy.wait_recv()
-
-    for k in range(CHUNKS):
+            t_copies.append(copy)
+        tri_all[ch, k, me] = tri_send[k, me]
+        forward(k, dests - 1, me)
+
+    def forward(k, slot, source):
+        copy = pltpu.make_async_remote_copy(
+            src_ref=tri_all.at[ch, k, source],
+            dst_ref=tri_all.at[ch, k, source],
+            send_sem=f_send.at[k, slot],
+            recv_sem=f_recv.at[k, slot],
+            device_id={"ch": other_ch},
+            device_id_type=MESH,
+        )
+        copy.start()
+        f_copies[k].append(copy)
+
+    def forward_all(k):
+        for p in range(dests - 1):
+            t_copies[k * (dests - 1) + p].wait_recv()
+            forward(k, p, peers[p][0])
+
+    def finish(k):
+        for copy in f_copies[k]:
+            copy.wait_recv()
         cells = pl.ds(k * width, width)
         parts = []
-        for t in range(k * per, (k + 1) * per, 2):
-            evens, odds = [], []
-            for c in range(2):
-                for q in range(dests):
-                    one = tri_all[c, 0, q, t * 4 : t * 4 + 8, :].astype(jnp.float32)
-                    two = tri_all[c, 1, q, t * 4 : t * 4 + 8, :].astype(jnp.float32)
-                    evens.append(jnp.where(upper, one, pltpu.roll(two, 4, 0)))
-                    odds.append(jnp.where(upper, pltpu.roll(one, 4, 0), two))
-            parts.append(jnp.concatenate(evens, axis=0))
-            parts.append(jnp.concatenate(odds, axis=0))
+        for t in range(per):
+            stack = [
+                tri_all[c, k, q, t * 8 : t * 8 + 8, :].astype(jnp.float32)
+                for c in range(2)
+                for q in range(dests)
+            ]
+            parts.append(jnp.concatenate(stack, axis=0))
         post = normalise(jnp.concatenate(parts, axis=1), post_gain_wide, post_shift_wide)
         update = jnp.dot(weights[5 * HALF :, :], post, preferred_element_type=jnp.float32)
         o_ref[:, cells] = (update * gate_keep[:, cells]).astype(jnp.bfloat16)
-    for copy in x_copies + a_copies[0] + a_copies[1] + t_copies[0] + t_copies[1] + f_copies:
+
+    for k in range(CHUNKS):
+        f_copies.append([])
+        products(k)
+        if k > 1:
+            forward_all(k - 2)
+    for k in range(CHUNKS - 2, CHUNKS):
+        forward_all(k)
+        finish(k - 2)
+    finish(CHUNKS - 2)
+    finish(CHUNKS - 1)
+    for copy in x_copies + a_copies[0] + a_copies[1] + t_copies + sum(f_copies, []):
         copy.wait_send()
 
 
@@ -384,6 +386,7 @@
     chan, slab_rows, slab_cols = pair_act.shape
     cells = slab_rows * slab_cols
     tiles = cells // LANES
+    block = tiles // CHUNKS * 8
     flat = pair_act.reshape(chan, cells)
     vmem = pl.BlockSpec(memory_space=pltpu.VMEM)
     sems = pltpu.SemaphoreType.DMA
@@ -396,26 +399,25 @@
             pltpu.VMEM((2 * chan, cells), jnp.bfloat16),
             pltpu.VMEM((6 * HALF, LANES), jnp.bfloat16),
             pltpu.VMEM((768, LANES), jnp.float32),
-            pltpu.VMEM((4 * HALF, LANES), jnp.float32),
             pltpu.VMEM((LANES, LANES), jnp.float32),
             pltpu.VMEM((chan, cells), jnp.float32),
             pltpu.VMEM((2, dests, tiles * 8, LANES), jnp.bfloat16),
             pltpu.VMEM((2, dests, tiles * 8, LANES), jnp.bfloat16),
-            pltpu.VMEM((2, tiles * 8, LANES), jnp.float32),
-            pltpu.VMEM((2, 4, LANES, LANES), jnp.bfloat16),
-            pltpu.VMEM((4, LANES, LANES), jnp.float32),
-            pltpu.VMEM((dests, tiles * 4, LANES), jnp.float32),
-            pltpu.VMEM((2, dests, tiles * 4, LANES), jnp.bfloat16),
-            pltpu.VMEM((2, 2, dests, tiles * 4, LANES), jnp.bfloat16),
+            pltpu.VMEM((2, max(tiles * 8, rows * block), LANES), jnp.float32),
+            pltpu.VMEM((8, LANES, LANES), jnp.bfloat16),
+            pltpu.VMEM((8, LANES, LANES), jnp.float32),
+            pltpu.VMEM((2, rows * block, LANES), jnp.float32),
+            pltpu.VMEM((CHUNKS, dests, block, LANES), jnp.bfloat16),
+            pltpu.VMEM((2, CHUNKS, dests, block, LANES), jnp.bfloat16),
             sems,
             sems((CHUNKS,)),
             sems((CHUNKS,)),
             sems((2, dests, CHUNKS)),
             sems((2, dests, CHUNKS)),
-            sems((2, dests)),
-            sems((2, dests)),
-            sems((2, dests)),
-            sems((2, dests)),
+            sems((CHUNKS, dests)),
+            sems((CHUNKS, dests)),
+            sems((CHUNKS, dests)),
+            sems((CHUNKS, dests)),
         ],
         compiler_params=pltpu.CompilerParams(
             collective_id=0, has_side_effects=True, vmem_limit_bytes=32 * 1024 * 1024

time: 38.2 us -> 36.9 us (0.966)
  Pallas kernels: 35 us -> 33.7 us
    pallas_call x1, Pallas kernels: 35 us -> 33.7 us  [fused_body(): pl.pallas_call(functools.partial(fused_kernel, rows), out_shape=jax.Shape...]
where the time goes in v3:
time: 36.9 us; the launch traced here: 36.7 us
  Pallas kernels  33.7 us (91%)
  local copies, waits for them, and re-layouts  2.96 us (8%)
    pallas_call x1, Pallas kernels, fused_body(): pl.pallas_call(functools.partial(fused_kernel, rows), out_shape=jax.Shape...  33.7 us
    reshape x1, local copies, waits for them, and re-layouts, fused_body(): flat = pair_act.reshape(chan, cells)  1.61 us
    reshape x1, local copies, waits for them, and re-layouts, fused_body(): return out.reshape(pair_act.shape)  1.31 us

profile of v3, /device:TPU:0, one launch (start us, length us, event | category | flops | bytes accessed | tf_op | source)
XLA Modules:
  0.0 36.7 jit_solution(2468004545493243348)
XLA Ops:
  0.0 0.0 copy-start
  0.0 0.0 copy-start.1
  0.0 0.0 copy-start.2
  0.0 0.0 copy-start.3
  0.0 0.0 copy-start.4
  0.0 0.0 copy-start.5
  0.0 0.0 copy-start.6
  0.0 0.0 copy-start.7
  0.0 0.0 copy-start.8
  0.1 1.6 %reshape.21.x_ref = bf16[64,2048]{1,0:T(8,128)(2,1)S(1)} reshape(bf16[64,32,64]{2,1,0:T(8,128)(2,1)} %param.10) | data formatting | bytes 524288 | tf_op jit(solution)/shard_map/reshape | solution.py:390
  1.7 0.0 copy-done
  1.7 0.0 copy-done.1
  1.7 0.0 copy-done.2
  1.7 0.0 copy-done.3
  1.7 0.0 copy-done.4
  1.7 0.0 copy-done.5
  1.7 0.0 copy-done.6
  1.7 0.0 copy-done.7
  1.7 0.0 copy-done.8
  1.8 33.7 %triangle_update.1 = bf16[64,2048]{1,0:T(8,128)(2,1)S(1)} custom-call(bf16[64,2048]{1,0:T(8,128)(2,1)S(1)} %reshape.21.x_ref, s32[1,128]{1,0:T(1,128)S(1)} %bitcast.5, f32[1,128]{1,0:T(1,128)S(1)} %bitcast.6, f32[1,128]{1,0:T(1,128)S(1)} %bitcast.7, bf16[128,256]{1,0:T(8,128)(2,1)S(1)} %copy-done, bf16[128,256]{1,0:T(8,128)(2,1)S(1)} %copy-done.1, ...), custom_call_target="tpu_custom_call" | custom-call | tf_op jit(solution)/shard_map/triangle_update/pallas_call | solution.py:393
  35.4 1.3 %reshape.27 = bf16[64,32,64]{2,1,0:T(8,128)(2,1)} reshape(bf16[64,2048]{1,0:T(8,128)(2,1)S(1)} %triangle_update.1) | data formatting | bytes 524288 | tf_op jit(solution)/shard_map/reshape | solution.py:438
Async XLA Ops:
  0.0 1.7 %copy-start = (bf16[128,256]{1,0:T(8,128)(2,1)S(1)}, bf16[128,256]{1,0:T(8,128)(2,1)}, u32[]{:S(2)}) copy-start(bf16[128,256]{1,0:T(8,128)(2,1)} %proj_ref.1) | copy-start | bytes 196612
  0.0 1.7 %copy-start.1 = (bf16[128,256]{1,0:T(8,128)(2,1)S(1)}, bf16[128,256]{1,0:T(8,128)(2,1)}, u32[]{:S(2)}) copy-start(bf16[128,256]{1,0:T(8,128)(2,1)} %gate_ref.1) | copy-start | bytes 196612
  0.0 1.7 %copy-start.2 = (bf16[128,128]{1,0:T(8,128)(2,1)S(1)}, bf16[128,128]{1,0:T(8,128)(2,1)}, u32[]{:S(2)}) copy-start(bf16[128,128]{1,0:T(8,128)(2,1)} %outgate_ref.1) | copy-start | bytes 98308
  0.0 1.7 %copy-start.3 = (bf16[128,128]{1,0:T(8,128)(2,1)S(1)}, bf16[128,128]{1,0:T(8,128)(2,1)}, u32[]{:S(2)}) copy-start(bf16[128,128]{1,0:T(8,128)(2,1)} %out_weight.1) | copy-start | bytes 98308
  0.0 1.7 %copy-start.4 = (s32[128]{0:T(128)S(1)}, s32[128]{0:T(128)}, u32[]{:S(2)}) copy-start(s32[128]{0:T(128)} %param.11) | copy-start | bytes 1540
  0.0 1.7 %copy-start.5 = (f32[128]{0:T(128)S(1)}, f32[128]{0:T(128)}, u32[]{:S(2)}) copy-start(f32[128]{0:T(128)} %param.12) | copy-start | bytes 1540
  0.0 1.7 %copy-start.6 = (f32[128]{0:T(128)S(1)}, f32[128]{0:T(128)}, u32[]{:S(2)}) copy-start(f32[128]{0:T(128)} %param.13) | copy-start | bytes 1540
  0.0 1.7 %copy-start.7 = (f32[128]{0:T(128)S(1)}, f32[128]{0:T(128)}, u32[]{:S(2)}) copy-start(f32[128]{0:T(128)} %param.17) | copy-start | bytes 1540
  0.0 1.7 %copy-start.8 = (f32[128]{0:T(128)S(1)}, f32[128]{0:T(128)}, u32[]{:S(2)}) copy-start(f32[128]{0:T(128)} %param.18) | copy-start | bytes 1540
